TPU v7x, 32 devices: a whole 2x2x4 slice. The times are simulated.
32 devices in a mesh: parts: 2 (over x), rep: 16 (over z, y, core), tp: 1.
Axes of the slice: x: 2, y: 2, z: 4, core: 2. Of those that a mesh axis runs over, the one named last changes fastest.
Arguments:
- hidden: bfloat16 [8192, 8192], P(('parts', 'rep'), 'tp'), parts along dimension 0, may hold values from -6 to 6
- request_adapter: int32 [8192, 1], P(('parts', 'rep')), parts along dimension 0, may hold values from 0 to 31; in each aligned block of 256 rows (0 to 255, 256 to 511, ...) at most 24 rows name the same one
- lengths: int32 [8192], P(('parts', 'rep')), parts along dimension 0, may hold values from 1 to 4096
- key_projection_weight: bfloat16 [8192, 1024], P('tp'), may hold values from -0.0625 to 0.0625
- adapter_down_weight: bfloat16 [32, 8192, 128], P('rep', 'tp'), may hold values from -0.0625 to 0.0625
- adapter_up_weight: bfloat16 [32, 128, 1024], P('rep', None, 'tp'), may hold values from -3 to 3
- slot_adapter_rank: int32 [32], P('rep'), may hold values from 16 to 128, as said below
- placement: int32 [32], replicated, may hold values from 0 to 31, each once
Outputs:
- new_keys: bfloat16 [8192, 1024], P(('parts', 'rep'), 'tp'), parts along dimension 0
There are 2 independent parts, one for each index of `parts`. A program takes and returns all parts, laid end to end along the dimension named above; an argument that names none is the same for every part. Nothing has to cross between parts.
Inputs may be any that keep to these rules, and one draw needn't show every extreme that they name: `slot_adapter_rank`: each slot holds a power of two. `request_adapter`: at most 24 of the 256 requests of one replica name one adapter, a bound that some block reaches of them.
All inputs are finite; a program needn't handle non-finite values.
Results may differ from a plain program's by a relative error of at most 0.0039.
Values may be sent and summed in bfloat16 or wider, within the bound.
A program may use at most 128 MiB of HBM per device.

v0:
```python
import math

import jax
import jax.numpy as jnp
from jax import lax
from jax.sharding import PartitionSpec as P

HEAD = 128


def rotary(values, positions, head_size):
    row_count = values.shape[0]
    grouped = values.reshape(row_count, -1, head_size)
    half_size = head_size // 2
    inverse = jnp.exp(
        jnp.arange(half_size, dtype=jnp.float32) * (-2.0 * math.log(10000.0) / head_size)
    )
    angles = positions.astype(jnp.float32)[:, None] * inverse[None, :]
    cosine = jnp.cos(angles)[:, None, :]
    sine_part = jnp.sin(angles)[:, None, :]
    first_half = grouped[..., :half_size]
    second = grouped[..., half_size:]
    rotated = jnp.concatenate(
        [first_half * cosine - second * sine_part, second * cosine + first_half * sine_part],
        axis=-1,
    )
    return rotated.reshape(row_count, -1)


def on_device(
    hidden,
    request_adapter,
    lengths,
    key_projection_weight,
    adapter_down_weight,
    adapter_up_weight,
    slot_adapter_rank,
    placement,
):
    row_count = hidden.shape[0]
    feature_half = hidden.shape[1]
    adapter_number = placement.shape[0]
    replica_slot_list = adapter_down_weight.shape[0]
    rank_extent = adapter_down_weight.shape[2]
    key_portion = adapter_up_weight.shape[2]
    replicas = lax.axis_size("rep")
    slot_capacity = 3 * row_count // adapter_number
    table_hit = request_adapter == jnp.arange(adapter_number, dtype=jnp.int32)[None, :]
    slot_ids = jnp.sum(jnp.where(table_hit, placement[None, :], 0), axis=1)
    slot_hit = (slot_ids[:, None] == jnp.arange(adapter_number, dtype=jnp.int32)[None, :]).astype(
        jnp.int32
    )
    within = jnp.sum((jnp.cumsum(slot_hit, axis=0) - 1) * slot_hit, axis=1)
    request_place = slot_ids * slot_capacity + within
    outgoing = (
        jnp.zeros((adapter_number * slot_capacity, feature_half), jnp.bfloat16)
        .at[request_place]
        .set(hidden)
    )
    outgoing = outgoing.reshape(replicas, replica_slot_list, slot_capacity, feature_half)
    rank_scale = lax.rsqrt(slot_adapter_rank.astype(jnp.float32))
    rank_keep = jnp.arange(rank_extent, dtype=jnp.int32)[None, :] < slot_adapter_rank[:, None]
    partial_value = jnp.dot(hidden, key_projection_weight, preferred_element_type=jnp.float32)
    received_rows = lax.all_to_all(outgoing, "rep", split_axis=0, concat_axis=0, tiled=True)
    summed = lax.psum(
        jnp.einsum(
            "khlt,htq->khlq", received_rows, adapter_down_weight, preferred_element_type=jnp.float32
        ),
        "tp",
    )
    reduced_rank_rows = jnp.where(
        rank_keep[None, :, None, :], summed * rank_scale[None, :, None, None], 0.0
    ).astype(jnp.bfloat16)
    sent_back_rows = lax.all_to_all(
        jnp.einsum(
            "pkwb,kbj->pkwj",
            reduced_rank_rows,
            adapter_up_weight,
            preferred_element_type=jnp.float32,
        ).astype(jnp.bfloat16),
        "rep",
        split_axis=0,
        concat_axis=0,
        tiled=True,
    )
    adapter_rows = sent_back_rows.reshape(adapter_number * slot_capacity, key_portion)[
        request_place
    ]
    summed_base = lax.psum(partial_value, "tp")
    replica_portion = lax.dynamic_slice_in_dim(
        summed_base, lax.axis_index("tp") * key_portion, key_portion, 1
    )
    key_output_rows = replica_portion + adapter_rows.astype(jnp.float32)
    return rotary(key_output_rows, lengths, HEAD).astype(jnp.bfloat16)


def solution(mesh):
    in_specs = (
        P(("parts", "rep"), "tp"),
        P(("parts", "rep"), None),
        P(("parts", "rep")),
        P("tp", None),
        P("rep", "tp", None),
        P("rep", None, "tp"),
        P("rep"),
        P(),
    )
    out_specs = P(("parts", "rep"), "tp")
    return jax.shard_map(
        on_device, mesh=mesh, in_specs=in_specs, out_specs=out_specs, check_vma=False
    )
```

profile of v0, /device:TPU:13, one launch (start us, length us, event | category | flops | bytes accessed | tf_op | source)
XLA Modules:
  0.0 359.8 jit_solution(3529559969606505845)
XLA Ops:
  0.0 0.0 copy-start
  0.0 0.8 select_reduce_fusion
  0.9 0.6 reduce-window.6
  1.4 0.2 slice_reduce_fusion
  1.7 0.1 fusion.36
  1.8 14.5 %scatter_custom_fusion = bf16[768,8192]{1,0:T(8,128)(2,1)} fusion(s32[256]{0:T(256)S(1)} %bitcast.61, bf16[256,8192]{1,0:T(8,128)(2,1)} %param.8, bf16[]{:T(256)} %constant.7.clone.1), kind=kCustom, calls=%fused_computation.4 | custom fusion | bytes 12583424 | tf_op jit(solution)/shard_map/scatter | solution.py:58
  16.3 6.7 %all-to-all-start = ((bf16[16,2,24,8192]{3,2,1,0:T(8,128)(2,1)}), bf16[16,2,24,8192]{3,2,1,0:T(8,128)(2,1)}, u32[]{:S(2)}, u32[]{:S(2)}) async-start(bf16[16,2,24,8192]{3,2,1,0:T(8,128)(2,1)} %bitcast.56), calls=%async_computation | async-start | bytes 25165824 | tf_op jit(solution)/shard_map/all_to_all | solution.py:64
  23.0 0.0 copy-done.2
  23.0 0.1 iota_compare_fusion.3
  23.1 272.1 %all-to-all-done = bf16[16,2,24,8192]{3,2,1,0:T(8,128)(2,1)} async-done(((bf16[16,2,24,8192]{3,2,1,0:T(8,128)(2,1)}), bf16[16,2,24,8192]{3,2,1,0:T(8,128)(2,1)}, u32[]{:S(2)}, u32[]{:S(2)}) %all-to-all-start) | async-done | bytes 12582944 | tf_op jit(solution)/shard_map/all_to_all | solution.py:64
  295.2 0.0 copy-done
  295.2 9.7 %fusion.5 = bf16[16,2,24,1024]{3,2,0,1:T(8,128)(2,1)S(1)} fusion(bf16[2,8192,128]{2,1,0:T(8,128)(2,1)} %param.12, bf16[16,2,24,8192]{3,2,1,0:T(8,128)(2,1)} %all-to-all-done, bf16[2,128,1024]{2,1,0:T(8,128)(2,1)S(1)} %copy-done, f32[2]{0:T(128)S(1)} %convert_rsqrt_fusion, pred[2,128]{1,0:T(4,128)(4,1)S(1)} %iota_compare_fusion.3), kind=kOutput, calls=%fused_computation.8 | convolution fusion | flops 1813020672 | bytes 18874632 | tf_op jit(solution)/shard_map/pkwb,kbj->pkwj/dot_general | solution.py:75
  304.9 0.0 copy-start.1
  304.9 1.3 copy.18
  306.2 4.9 %all-to-all-start.1 = ((bf16[16,2,24,1024]{3,2,1,0:T(8,128)(2,1)}), bf16[16,2,24,1024]{3,2,1,0:T(8,128)(2,1)S(1)}, u32[]{:S(2)}, u32[]{:S(2)}) async-start(bf16[16,2,24,1024]{3,2,1,0:T(8,128)(2,1)} %copy.18), calls=%async_computation.1 | async-start | bytes 3145728 | tf_op jit(solution)/shard_map/all_to_all | solution.py:74
  311.1 0.0 copy-done.1
  311.1 0.5 multiply_cosine_fusion
  311.6 35.6 %all-to-all-done.1 = bf16[16,2,24,1024]{3,2,1,0:T(8,128)(2,1)S(1)} async-done(((bf16[16,2,24,1024]{3,2,1,0:T(8,128)(2,1)}), bf16[16,2,24,1024]{3,2,1,0:T(8,128)(2,1)S(1)}, u32[]{:S(2)}, u32[]{:S(2)}) %all-to-all-start.1) | async-done | bytes 1572896 | tf_op jit(solution)/shard_map/all_to_all | solution.py:74
  347.3 1.2 gather_fusion
  348.4 9.5 %fusion.6 = f32[32,8,8,128]{3,1,2,0:T(8,128)S(1)} fusion(bf16[256,8192]{1,0:T(8,128)(2,1)} %param.8, bf16[8192,1024]{1,0:T(8,128)(2,1)} %param.11, bf16[256,1024]{1,0:T(8,128)(2,1)S(1)} %gather_fusion), kind=kOutput, calls=%fused_computation.10 | convolution fusion | flops 4295491584 | bytes 22544384 | tf_op jit(solution)/shard_map/dot_general | solution.py:63
  357.9 0.2 copy.22
  358.1 0.5 subtract_convert_fusion
  358.6 0.3 pad_maximum_fusion
  358.9 0.9 copy.38
  (10 shorter events, 0.1 us)
Async XLA Ops:
  0.0 295.2 %copy-start = (bf16[2,128,1024]{2,1,0:T(8,128)(2,1)S(1)}, bf16[2,128,1024]{2,1,0:T(8,128)(2,1)}, u32[]{:S(2)}) copy-start(bf16[2,128,1024]{2,1,0:T(8,128)(2,1)} %param.13) | copy-start | bytes 1572868
  16.3 6.7 %copy-start.2 = (s32[2]{0:T(128)S(1)}, s32[2]{0:T(128)}, u32[]{:S(2)}) copy-start(s32[2]{0:T(128)} %param.14) | copy-start | bytes 28
  16.3 278.9 %all-to-all-start = ((bf16[16,2,24,8192]{3,2,1,0:T(8,128)(2,1)}), bf16[16,2,24,8192]{3,2,1,0:T(8,128)(2,1)}, u32[]{:S(2)}, u32[]{:S(2)}) async-start(bf16[16,2,24,8192]{3,2,1,0:T(8,128)(2,1)} %bitcast.56), calls=%async_computation | async-start | bytes 25165824 | tf_op jit(solution)/shard_map/all_to_all | solution.py:64
  304.9 6.2 %copy-start.1 = (s32[256]{0:T(256)S(1)}, s32[256]{0:T(256)}, u32[]{:S(2)}) copy-start(s32[256]{0:T(256)} %param.10) | copy-start | bytes 3076
  306.2 41.1 %all-to-all-start.1 = ((bf16[16,2,24,1024]{3,2,1,0:T(8,128)(2,1)}), bf16[16,2,24,1024]{3,2,1,0:T(8,128)(2,1)S(1)}, u32[]{:S(2)}, u32[]{:S(2)}) async-start(bf16[16,2,24,1024]{3,2,1,0:T(8,128)(2,1)} %copy.18), calls=%async_computation.1 | async-start | bytes 3145728 | tf_op jit(solution)/shard_map/all_to_all | solution.py:74
where the time goes:
time: 360 us
  waiting for transfers between devices  308 us (86%)
  matrix products  19.1 us (5%)
  local copies, waits for them, and re-layouts  18.2 us (5%)
  starting transfers between devices  11.6 us (3%)
    all_to_all x1, waiting for transfers between devices, on_device(): lax.all_to_all(outgoing, 'rep', split_axis=0, concat_axis=0, tiled=True)  272 us
    all_to_all x1, waiting for transfers between devices, on_device(): lax.all_to_all(jnp.einsum('pkwb,kbj->pkwj', reduced_rank_rows, adapter_up...  35.6 us
    scatter x1, local copies, waits for them, and re-layouts, on_device(): outgoing = jnp.zeros((adapter_number * slot_capacity, feature_half), jnp....  14.5 us
    dot_general x1, matrix products, on_device(): jnp.einsum('pkwb,kbj->pkwj', reduced_rank_rows, adapter_up_weight, prefer...  9.66 us
    dot_general x1, matrix products, on_device(): jnp.dot(hidden, key_projection_weight, preferred_element_type=jnp.float32)  9.46 us
  transfers between devices with their start and end apart: 2, of which 2 were waited for; matrix products, arithmetic and copies ran while one was open for 0% of the time, Pallas kernels for 0%

commit v1 on v0

--- a/solution.py
+++ b/solution.py
@@ -1,8 +1,11 @@
+import functools
 import math
 
 import jax
 import jax.numpy as jnp
 from jax import lax
+from jax.experimental import pallas as pl
+from jax.experimental.pallas import tpu as pltpu
 from jax.sharding import PartitionSpec as P
 
 HEAD = 128
@@ -27,7 +30,7 @@
     return rotated.reshape(row_count, -1)
 
 
-def on_device(
+def routed(
     hidden,
     request_adapter,
     lengths,
@@ -94,7 +97,366 @@
     return rotary(key_output_rows, lengths, HEAD).astype(jnp.bfloat16)
 
 
+MESH = pl.DeviceIdType.MESH
+LAG = 4
+
+
+def shrink_kernel(
+    n,
+    group,
+    hidden,
+    key_weight,
+    down,
+    slots,
+    shrink,
+    base,
+    hidden_own,
+    key_buf,
+    hidden_got,
+    slots_got,
+    down_got,
+    total,
+    parts_got,
+    h_send,
+    h_recv,
+    s_send,
+    s_recv,
+    w_send,
+    w_recv,
+    f_send,
+    f_recv,
+    r_send,
+    r_recv,
+    own_sem,
+    key_sem,
+):
+    part = lax.axis_index("parts")
+    me = lax.axis_index("rep")
+    place = me % group
+    first = me - place
+    rows = hidden.shape[0]
+    width = hidden.shape[1] // group
+    depth = hidden.shape[1] // n
+    twin = 1 - part
+
+    def device(p, r):
+        return (p, r, 0)
+
+    def cols(j):
+        return pl.ds(pl.multiple_of(j * width, width), width)
+
+    def block(j):
+        return pl.ds(pl.multiple_of(j * rows, rows), rows)
+
+    barrier = pltpu.get_barrier_semaphore()
+    for k in range(1, n):
+        pl.semaphore_signal(
+            barrier, inc=1, device_id=device(part, (me + k) % n), device_id_type=MESH
+        )
+    pl.semaphore_signal(barrier, inc=1, device_id=device(twin, me), device_id_type=MESH)
+
+    own_hidden = pltpu.make_async_copy(hidden, hidden_own, own_sem.at[0])
+    own_cols = pltpu.make_async_copy(
+        hidden.at[:, cols(place)], hidden_got.at[block(place)], own_sem.at[1]
+    )
+    own_down = pltpu.make_async_copy(
+        down.at[:, cols(place)], down_got.at[pl.ds(2 * me, 2)], own_sem.at[2]
+    )
+    own_slots = pltpu.make_async_copy(slots, slots_got.at[block(place)], own_sem.at[3])
+
+    def key_copy(k):
+        at = pl.ds(pl.multiple_of(k * depth, depth), depth)
+        return pltpu.make_async_copy(key_weight.at[at], key_buf.at[at], key_sem.at[k])
+
+    def send_hidden(k):
+        to = (place + k) % group
+        return pltpu.make_async_remote_copy(
+            src_ref=hidden.at[:, cols(to)],
+            dst_ref=hidden_got.at[block(place)],
+            send_sem=h_send.at[k],
+            recv_sem=h_recv.at[place],
+            device_id=device(part, first + to),
+            device_id_type=MESH,
+        )
+
+    def send_slots(k):
+        to = (place + k) % group
+        return pltpu.make_async_remote_copy(
+            src_ref=slots,
+            dst_ref=slots_got.at[block(place)],
+            send_sem=s_send.at[k],
+            recv_sem=s_recv.at[place],
+            device_id=device(part, first + to),
+            device_id_type=MESH,
+        )
+
+    def send_down(k):
+        to = (me + k) % n
+        return pltpu.make_async_remote_copy(
+            src_ref=down.at[part, cols(to % group)],
+            dst_ref=down_got.at[2 * me + part],
+            send_sem=w_send.at[k],
+            recv_sem=w_recv.at[me],
+            device_id=device(part, to),
+            device_id_type=MESH,
+        )
+
+    def pass_on(k):
+        source = (me + n - k) % n
+        return pltpu.make_async_remote_copy(
+            src_ref=down_got.at[2 * source + part],
+            dst_ref=down_got.at[2 * source + part],
+            send_sem=f_send.at[k],
+            recv_sem=f_recv.at[k],
+            device_id=device(twin, me),
+            device_id_type=MESH,
+        )
+
+    def got_hidden(k):
+        source = (place + k) % group
+        return pltpu.make_async_remote_copy(
+            src_ref=hidden.at[:, cols(place)],
+            dst_ref=hidden_got.at[block(source)],
+            send_sem=h_send.at[k],
+            recv_sem=h_recv.at[source],
+            device_id=device(part, first + source),
+            device_id_type=MESH,
+        )
+
+    def got_slots(k):
+        source = (place + k) % group
+        return pltpu.make_async_remote_copy(
+            src_ref=slots,
+            dst_ref=slots_got.at[block(source)],
+            send_sem=s_send.at[k],
+            recv_sem=s_recv.at[source],
+            device_id=device(part, first + source),
+            device_id_type=MESH,
+        )
+
+    def got_down(k):
+        source = (me + n - k) % n
+        return pltpu.make_async_remote_copy(
+            src_ref=down.at[part, cols(place)],
+            dst_ref=down_got.at[2 * source + part],
+            send_sem=w_send.at[k],
+            recv_sem=w_recv.at[source],
+            device_id=device(part, source),
+            device_id_type=MESH,
+        )
+
+    def got_passed(k):
+        source = (me + n - k) % n
+        return pltpu.make_async_remote_copy(
+            src_ref=down_got.at[2 * source + twin],
+            dst_ref=down_got.at[2 * source + twin],
+            send_sem=f_send.at[k],
+            recv_sem=f_recv.at[k],
+            device_id=device(twin, me),
+            device_id_type=MESH,
+        )
+
+    own_hidden.start()
+    for k in range(n):
+        key_copy(k).start()
+    own_down.start()
+    own_cols.start()
+    own_slots.start()
+    pl.semaphore_wait(barrier, n)
+    for k in range(1, group):
+        send_slots(k).start()
+    for k in range(1, n):
+        send_down(k).start()
+        if k < group:
+            send_hidden(k).start()
+
+    total[...] = jnp.zeros_like(total)
+    base[...] = jnp.zeros_like(base)
+    own_hidden.wait()
+
+    def base_step(k):
+        key_copy(k).wait()
+        at = pl.ds(pl.multiple_of(k * depth, depth), depth)
+        base[...] += jnp.dot(
+            hidden_own[:, at], key_buf[at, :], preferred_element_type=jnp.float32
+        )
+
+    def shrink_step(k):
+        source = (me + n - k) % n
+        low_slot = (2 * source).astype(jnp.float32)
+
+        def tile(j, carry):
+            at = block(j)
+            weight = jnp.concatenate([down_got[2 * source], down_got[2 * source + 1]], axis=1)
+            product = jnp.dot(hidden_got[at, :], weight, preferred_element_type=jnp.float32)
+            slot = slots_got[at, :].astype(jnp.float32)
+            half = product.shape[1] // 2
+            total[at, :] = jnp.where(
+                slot == low_slot,
+                product[:, :half],
+                jnp.where(slot == low_slot + 1.0, product[:, half:], total[at, :]),
+            )
+            return carry
+
+        lax.fori_loop(0, group, tile, 0)
+
+    base_step(0)
+
+    def early(k, carry):
+        got_down(k).wait_recv()
+        pass_on(k).start()
+        base_step(k)
+        return carry
+
+    def middle(k, carry):
+        got_down(k).wait_recv()
+        pass_on(k).start()
+        base_step(k)
+        got_passed(k - LAG).wait_recv()
+        shrink_step(k - LAG)
+        return carry
+
+    def late(k, carry):
+        got_passed(k).wait_recv()
+        shrink_step(k)
+        return carry
+
+    lax.fori_loop(1, LAG + 1, early, 0)
+    own_cols.wait()
+    own_down.wait()
+    own_slots.wait()
+    for k in range(1, group):
+        got_slots(k).wait_recv()
+        got_hidden(k).wait_recv()
+    shrink_step(0)
+    lax.fori_loop(LAG + 1, n, middle, 0)
+    lax.fori_loop(n - LAG, n, late, 0)
+
+    def send_total(k):
+        to = (place + k) % group
+        return pltpu.make_async_remote_copy(
+            src_ref=total.at[block(to)],
+            dst_ref=parts_got.at[place],
+            send_sem=r_send.at[k],
+            recv_sem=r_recv.at[place],
+            device_id=device(part, first + to),
+            device_id_type=MESH,
+        )
+
+    def got_total(k):
+        source = (place + k) % group
+        return pltpu.make_async_remote_copy(
+            src_ref=total.at[block(place)],
+            dst_ref=parts_got.at[source],
+            send_sem=r_send.at[k],
+            recv_sem=r_recv.at[source],
+            device_id=device(part, first + source),
+            device_id_type=MESH,
+        )
+
+    for k in range(1, group):
+        send_total(k).start()
+    summed = total[block(place), :]
+    for k in range(1, group):
+        got_total(k).wait_recv()
+        summed = summed + parts_got[(place + k) % group]
+    shrink[...] = summed
+
+    for k in range(1, group):
+        send_slots(k).wait_send()
+        send_hidden(k).wait_send()
+        send_total(k).wait_send()
+    for k in range(1, n):
+        send_down(k).wait_send()
+        pass_on(k).wait_send()
+
+
+def shrink_and_base(hidden, key_weight, down, slots):
+    n = lax.axis_size("rep")
+    group = n // 2
+    rows, features = hidden.shape
+    rank_extent = down.shape[2]
+    width = features // group
+    keys = key_weight.shape[1]
+    any_space = pl.BlockSpec(memory_space=pl.ANY)
+    vmem = pl.BlockSpec(memory_space=pltpu.VMEM)
+    dma = pltpu.SemaphoreType.DMA
+    return pl.pallas_call(
+        functools.partial(shrink_kernel, n, group),
+        out_shape=(
+            jax.ShapeDtypeStruct((rows, rank_extent), jnp.float32),
+            jax.ShapeDtypeStruct((rows, keys), jnp.float32),
+        ),
+        in_specs=[any_space] * 4,
+        out_specs=(vmem, vmem),
+        scratch_shapes=[
+            pltpu.VMEM((rows, features), jnp.bfloat16),
+            pltpu.VMEM((features, keys), jnp.bfloat16),
+            pltpu.VMEM((group * rows, width), jnp.bfloat16),
+            pltpu.VMEM((group * rows, rank_extent), jnp.bfloat16),
+            pltpu.VMEM((2 * n, width, rank_extent), jnp.bfloat16),
+            pltpu.VMEM((group * rows, rank_extent), jnp.float32),
+            pltpu.VMEM((group, rows, rank_extent), jnp.float32),
+            dma((group,)),
+            dma((group,)),
+            dma((group,)),
+            dma((group,)),
+            dma((n,)),
+            dma((n,)),
+            dma((n,)),
+            dma((n,)),
+            dma((group,)),
+            dma((group,)),
+            dma((4,)),
+            dma((n,)),
+        ],
+        compiler_params=pltpu.CompilerParams(
+            collective_id=0, has_side_effects=True, vmem_limit_bytes=56 * 2**20
+        ),
+        cost_estimate=pl.CostEstimate(
+            flops=2 * rows * features * keys + 4 * rows * features * n * rank_extent,
+            bytes_accessed=2 * features * (rows + keys + 2 * rank_extent),
+            transcendentals=0,
+        ),
+    )(hidden, key_weight, down, slots)
+
+
+def shared(
+    hidden,
+    request_adapter,
+    lengths,
+    key_projection_weight,
+    adapter_down_weight,
+    adapter_up_weight,
+    slot_adapter_rank,
+    placement,
+):
+    rows = hidden.shape[0]
+    adapters = placement.shape[0]
+    rank_extent = adapter_down_weight.shape[2]
+    numbers = jnp.arange(adapters, dtype=jnp.int32)[None, :]
+    slot_ids = jnp.sum(jnp.where(request_adapter == numbers, placement[None, :], 0), axis=1)
+    slot_hit = slot_ids[:, None] == numbers
+    slots = jnp.broadcast_to(slot_ids[:, None].astype(jnp.bfloat16), (rows, rank_extent))
+    all_up = lax.all_gather(adapter_up_weight, "rep", tiled=True)
+    all_ranks = lax.all_gather(slot_adapter_rank, "rep", tiled=True)
+    shrink, base = shrink_and_base(hidden, key_projection_weight, adapter_down_weight, slots)
+    rank = jnp.sum(jnp.where(slot_hit, all_ranks[None, :], 0), axis=1)[:, None]
+    keep = jnp.arange(rank_extent, dtype=jnp.int32)[None, :] < rank
+    low = jnp.where(keep, shrink * lax.rsqrt(rank.astype(jnp.float32)), 0.0).astype(jnp.bfloat16)
+    spread = jnp.where(slot_hit[:, :, None], low[:, None, :], jnp.bfloat16(0))
+    delta = jnp.dot(
+        spread.reshape(rows, adapters * rank_extent),
+        all_up.reshape(adapters * rank_extent, -1),
+        preferred_element_type=jnp.float32,
+    ).astype(jnp.bfloat16)
+    return rotary(base + delta.astype(jnp.float32), lengths, HEAD).astype(jnp.bfloat16)
+
+
 def solution(mesh):
+    sizes = dict(mesh.shape)
+    fits = sizes["parts"] == 2 and sizes["tp"] == 1 and sizes["rep"] % 8 == 0
+    on_device = shared if fits else routed
     in_specs = (
         P(("parts", "rep"), "tp"),
         P(("parts", "rep"), None),

time: 360 us -> 253 us (0.70)
  waiting for transfers between devices: 308 us -> 0.73 us
  Pallas kernels: 0 us -> 216 us
  local copies, waits for them, and re-layouts: 18.2 us -> 3.92 us
  between operations: 0.12 us -> 14.1 us
  matrix products: 19.1 us -> 6.03 us
  starting transfers between devices: 11.6 us -> 0.01 us
  blocking collectives: 0 us -> 7.89 us
    all_to_all x2 -> x0, waiting for transfers between devices: 308 us -> none  [the longest x1 272 us: on_device(): lax.all_to_all(outgoing, 'rep', split_axis=0, concat_axis=0, tiled=True)]
    pallas_call x0 -> x1, Pallas kernels: none -> 216 us  [shrink_and_base(): pl.pallas_call(functools.partial(shrink_kernel, n, group), out_shape=(jax...]
    scatter x1 -> x0, local copies, waits for them, and re-layouts: 14.5 us -> none  [on_device(): outgoing = jnp.zeros((adapter_number * slot_capacity, feature_half), jnp....]
    dot_general x2 -> x1, matrix products: 19.1 us -> 6.03 us  [shared(): jnp.dot(spread.reshape(rows, adapters * rank_extent), all_up.reshape(adap...]
    all_to_all x2 -> x0, starting transfers between devices: 11.6 us -> none  [the longest x1 6.69 us: on_device(): lax.all_to_all(outgoing, 'rep', split_axis=0, concat_axis=0, tiled=True)]
    unnamed x0 -> x1, blocking collectives: none -> 7.89 us
  transfers between devices with their start and end apart: 2 -> 1, of which waited for: 2 -> 0; matrix products, arithmetic and copies ran while one was open for 0% -> 2% of each run, Pallas kernels for 0% -> 85%
where the time goes in v1:
time: 253 us
  Pallas kernels  216 us (85%)
  between operations  14.1 us (6%)
  blocking collectives  7.89 us (3%)
  matrix products  6.03 us (2%)
  other arithmetic  3.98 us (2%)
  local copies, waits for them, and re-layouts  3.92 us (2%)
    pallas_call x1, Pallas kernels, shrink_and_base(): pl.pallas_call(functools.partial(shrink_kernel, n, group), out_shape=(jax...  216 us
    unnamed x1, blocking collectives  7.89 us
    dot_general x1, matrix products, shared(): jnp.dot(spread.reshape(rows, adapters * rank_extent), all_up.reshape(adap...  6.03 us
  transfers between devices with their start and end apart: 1, of which 0 were waited for; matrix products, arithmetic and copies ran while one was open for 2% of the time, Pallas kernels for 85%

profile of v1, /device:TPU:13, one launch (start us, length us, event | category | flops | bytes accessed | tf_op | source)
XLA Modules:
  0.0 252.7 jit_solution(4387156610001633226)
XLA Ops:
  6.5 0.0 all-gather.2.cloned.1.call-start
  6.5 0.7 all-gather.2.cloned.1.call-update
  7.3 0.8 select_reduce_fusion.1
  8.1 0.7 convert_element_type.37
  8.7 1.2 dynamic-slice
  10.6 0.9 dynamic-update-slice
  11.5 7.9 %all-reduce = s32[32]{0:T(128)S(1)} all-reduce(s32[32]{0:T(128)S(1)} %dynamic-update-slice), channel_id=1, replica_groups=mesh['parts'=2,'rep'=16,'tp'=1] {'rep'}, use_global_device_ids=true, to_apply=%add | all-reduce | flops 32 | bytes 256
  19.4 0.1 select_reduce_fusion
  19.5 0.7 broadcast_in_dim.62.slots
  20.2 216.0 %shard_map.82 = (f32[256,128]{1,0:T(8,128)}, f32[256,1024]{1,0:T(8,128)}) custom-call(bf16[256,8192]{1,0:T(8,128)(2,1)} %hidden.1, bf16[8192,1024]{1,0:T(8,128)(2,1)} %key_weight.1, bf16[2,8192,128]{2,1,0:T(8,128)(2,1)} %down.1, bf16[256,128]{1,0:T(8,128)(2,1)} %broadcast_in_dim.62.slots), custom_call_target="tpu_custom_call" | custom-call | flops 21474836480 | bytes 25165824 | tf_op jit(solution)/shard_map/pallas_call | solution.py:384
  236.3 1.0 select_convert_fusion
  237.3 0.5 multiply_cosine_fusion
  237.9 0.0 all-gather.2.cloned.1.call-done
  237.9 6.0 %fusion.15 = f32[32,8,8,128]{3,1,2,0:T(8,128)S(1)} fusion(f32[256,1024]{1,0:T(8,128)} %get-tuple-element.7, bf16[32,128,1024]{2,1,0:T(8,128)(2,1)} %all-gather.2.cloned.1.call-done, pred[256,32]{0,1:T(8,128)(4,1)S(1)} %iota_compare_fusion.1, bf16[256,128]{1,0:T(8,128)(2,1)S(1)} %select_convert_fusion), kind=kOutput, calls=%fused_computation.7 | convolution fusion | flops 2149318656 | bytes 10559488 | tf_op jit(solution)/shard_map/dot_general | solution.py:448
  243.9 0.2 copy.9
  244.1 0.5 subtract_convert_fusion
  244.7 0.3 pad_maximum_fusion
  245.0 0.9 copy.12
  (5 shorter events, 0.0 us)
Async XLA Ops:
  6.5 231.4 %all-gather.2.cloned.1.call-start = ((), (), s32[]{:S(2)}) async-start(), calls=%async_computation | async-start | bytes 8912896 | tf_op jit(solution)/shard_map/all_gather | solution.py:441
Sparse Core Ops, SparseCore 0:
  9.5 186.7 all-gather.1

commit v2 on v0

--- a/solution.py
+++ b/solution.py
@@ -1,8 +1,11 @@
+import functools
 import math
 
 import jax
 import jax.numpy as jnp
 from jax import lax
+from jax.experimental import pallas as pl
+from jax.experimental.pallas import tpu as pltpu
 from jax.sharding import PartitionSpec as P
 
 HEAD = 128
@@ -27,7 +30,7 @@
     return rotated.reshape(row_count, -1)
 
 
-def on_device(
+def routed(
     hidden,
     request_adapter,
     lengths,
@@ -94,7 +97,493 @@
     return rotary(key_output_rows, lengths, HEAD).astype(jnp.bfloat16)
 
 
+MESH = pl.DeviceIdType.MESH
+WINDOW = 4
+TILE = 1024
+TURN = 9
+
+
+def flip(index, mask):
+    out = 0
+    for bit in (1, 2, 4, 8):
+        out = out + (index // bit % 2 + mask // bit % 2) % 2 * bit
+    return out
+
+
+def mask_at(k):
+    return k % 2 * (8 + k // 2) + (1 - k % 2) * ((k // 2 * 4 + 6) % 7 + 1)
+
+
+def keys_kernel(
+    n,
+    group,
+    hidden,
+    key_weight,
+    down,
+    up,
+    slots,
+    cosine,
+    sine,
+    out,
+    hidden_own,
+    key_buf,
+    hidden_got,
+    slots_got,
+    down_got,
+    up_got,
+    base,
+    total,
+    totals_got,
+    low_got,
+    delta,
+    delta_got,
+    h_send,
+    h_recv,
+    s_send,
+    s_recv,
+    d_send,
+    d_recv,
+    dp_send,
+    dp_recv,
+    u_send,
+    u_recv,
+    up_send,
+    up_recv,
+    t_send,
+    t_recv,
+    l_send,
+    l_recv,
+    e_send,
+    e_recv,
+    own_sem,
+    key_sem,
+):
+    part = lax.axis_index("parts")
+    me = lax.axis_index("rep")
+    twin = 1 - part
+    place = me % group
+    first = me - place
+    rows, features = hidden.shape
+    rank_extent = down.shape[2]
+    width = features // group
+    depth = features // n
+    keys = key_weight.shape[1] // group
+
+    def part_of(j, size):
+        return pl.ds(pl.multiple_of(j * size, size), size)
+
+    def remote(source, target, send, recv, p, r):
+        return pltpu.make_async_remote_copy(
+            src_ref=source,
+            dst_ref=target,
+            send_sem=send,
+            recv_sem=recv,
+            device_id=(p, r, 0),
+            device_id_type=MESH,
+        )
+
+    def hidden_copy(k, to, who, other):
+        return remote(
+            hidden.at[:, part_of(to % group, width)],
+            hidden_got.at[part_of(who % group, rows)],
+            h_send.at[k],
+            h_recv.at[k],
+            part,
+            other,
+        )
+
+    def slots_copy(k, to, who, other):
+        return remote(
+            slots,
+            slots_got.at[part_of(who % group, rows)],
+            s_send.at[k],
+            s_recv.at[k],
+            part,
+            other,
+        )
+
+    def down_copy(k, to, who, other):
+        return remote(
+            down.at[part, part_of(to % group, width)],
+            down_got.at[2 * who + part],
+            d_send.at[k],
+            d_recv.at[k],
+            part,
+            other,
+        )
+
+    def near_copy(k, to, who, other):
+        return remote(
+            down.at[:, part_of(to % group, width)],
+            down_got.at[pl.ds(2 * who, 2)],
+            d_send.at[k],
+            d_recv.at[k],
+            part,
+            other,
+        )
+
+    def up_copy(k, to, who, other):
+        return remote(
+            up.at[part, :, part_of(to % group, keys)],
+            up_got.at[2 * who + part],
+            u_send.at[k],
+            u_recv.at[k],
+            part,
+            other,
+        )
+
+    def total_copy(k, to, who, other):
+        return remote(
+            total.at[part_of(to % group, rows)],
+            totals_got.at[who % group],
+            t_send.at[k],
+            t_recv.at[k],
+            part,
+            other,
+        )
+
+    def low_copy(k, to, who, other):
+        return remote(
+            low_got.at[who % group],
+            low_got.at[who % group],
+            l_send.at[k],
+            l_recv.at[k],
+            part,
+            other,
+        )
+
+    def delta_copy(k, to, who, other):
+        return remote(
+            delta.at[to % group],
+            delta_got.at[who % group],
+            e_send.at[k],
+            e_recv.at[k],
+            part,
+            other,
+        )
+
+    def sent(copy, k):
+        other = flip(me, k)
+        return copy(k, other, me, other)
+
+    def coming(copy, k):
+        other = flip(me, k)
+        return copy(k, me, other, other)
+
+    def down_pass(k, slot_part):
+        at = down_got.at[2 * flip(me, k) + slot_part]
+        return remote(at, at, dp_send.at[k], dp_recv.at[k], twin, me)
+
+    def up_pass(k, slot_part):
+        at = up_got.at[2 * flip(me, k) + slot_part]
+        return remote(at, at, up_send.at[k], up_recv.at[k], twin, me)
+
+    def key_copy(k):
+        at = part_of(k, depth)
+        return pltpu.make_async_copy(key_weight.at[at], key_buf.at[at], key_sem.at[k])
+
+    barrier = pltpu.get_barrier_semaphore()
+    for k in range(1, n):
+        pl.semaphore_signal(
+            barrier, inc=1, device_id=(part, flip(me, k), 0), device_id_type=MESH
+        )
+    pl.semaphore_signal(barrier, inc=1, device_id=(twin, me, 0), device_id_type=MESH)
+
+    own = [
+        pltpu.make_async_copy(hidden, hidden_own, own_sem.at[0]),
+        pltpu.make_async_copy(
+            hidden.at[:, part_of(place, width)],
+            hidden_got.at[part_of(place, rows)],
+            own_sem.at[1],
+        ),
+        pltpu.make_async_copy(
+            down.at[:, part_of(place, width)], down_got.at[pl.ds(2 * me, 2)], own_sem.at[2]
+        ),
+        pltpu.make_async_copy(
+            up.at[:, :, part_of(place, keys)], up_got.at[pl.ds(2 * me, 2)], own_sem.at[3]
+        ),
+        pltpu.make_async_copy(slots, slots_got.at[part_of(place, rows)], own_sem.at[4]),
+    ]
+    pl.semaphore_wait(barrier, n)
+    for k in range(1, WINDOW + 1):
+        sent(down_copy if k % 4 else near_copy, mask_at(k)).start()
+    for k in (1, 2, 3):
+        sent(hidden_copy, k).start()
+    for k in range(1, group):
+        sent(slots_copy, k).start()
+    for copy in own:
+        copy.start()
+    for k in range(n):
+        key_copy(k).start()
+
+    total[...] = jnp.zeros_like(total)
+    base[...] = jnp.zeros_like(base)
+
+    def base_step(k):
+        key_copy(k).wait()
+        at = part_of(k, depth)
+        base[...] += jnp.dot(
+            hidden_own[:, at], key_buf[at, :], preferred_element_type=jnp.float32
+        )
+
+    def pass_down(k):
+        mask = mask_at(k)
+
+        @pl.when(k % 4 > 0)
+        def _():
+            coming(down_copy, mask).wait_recv()
+            down_pass(mask, part).start()
+
+        @pl.when(k % 4 == 0)
+        def _():
+            coming(near_copy, mask).wait_recv()
+
+        later = k + WINDOW
+
+        @pl.when((later < n) & (later % 4 > 0))
+        def _():
+            sent(down_copy, mask_at(later)).start()
+
+        @pl.when((later < n) & (later % 4 == 0))
+        def _():
+            sent(near_copy, mask_at(later)).start()
+
+        base_step(k)
+
+    def shrink_pair(s):
+        low_slot = (2 * s).astype(jnp.float32)
+
+        def tile(j, carry):
+            at = part_of(j, TILE)
+            slot = slots_got[at, :].astype(jnp.float32)
+            weight = jnp.concatenate([down_got[2 * s], down_got[2 * s + 1]], axis=1)
+            product = jnp.dot(hidden_got[at, :], weight, preferred_element_type=jnp.float32)
+            total[at, :] = jnp.where(
+                slot == low_slot,
+                product[:, :rank_extent],
+                jnp.where(slot == low_slot + 1.0, product[:, rank_extent:], total[at, :]),
+            )
+            return carry
+
+        lax.fori_loop(0, group * rows // TILE, tile, 0)
+
+    def shrink_step(k, carry):
+        mask = mask_at(k)
+
+        @pl.when(k % 4 > 0)
+        def _():
+            down_pass(mask, twin).wait_recv()
+
+        shrink_pair(flip(me, mask))
+        return carry
+
+    def first_steps(k, carry):
+        pass_down(k)
+
+        @pl.when(k % 2 * (8 // (k + 1)) >= 1)
+        def _():
+            sent(hidden_copy, 4 + k // 2).start()
+
+        return carry
+
+    def last_steps(k, carry):
+        pass_down(k)
+        shrink_step(2 * (k - TURN) - 1, 0)
+        shrink_step(2 * (k - TURN), 0)
+        return carry
+
+    own[0].wait()
+    base_step(0)
+    lax.fori_loop(1, TURN + 1, first_steps, 0)
+    for k in range(1, n):
+        sent(up_copy, k).start()
+    for copy in own[1:]:
+        copy.wait()
+    for k in range(1, group):
+        coming(slots_copy, k).wait_recv()
+        coming(hidden_copy, k).wait_recv()
+    shrink_pair(me)
+    lax.fori_loop(TURN + 1, n, last_steps, 0)
+    lax.fori_loop(2 * (n - 1 - TURN) + 1, n, shrink_step, 0)
+    for k in range(1, group):
+        sent(total_copy, k).start()
+
+    def pass_up(k, carry):
+        mask = mask_at(k)
+        coming(up_copy, mask).wait_recv()
+        up_pass(mask, part).start()
+        return carry
+
+    lax.fori_loop(1, n, pass_up, 0)
+
+    def wait_passed_up(k, carry):
+        up_pass(mask_at(k), twin).wait_recv()
+        return carry
+
+    lax.fori_loop(1, n, wait_passed_up, 0)
+
+    own_slot = slots_got[part_of(place, rows), :].astype(jnp.float32)
+
+    def find_rank(s, rank):
+        here = up_got[s, rank_extent : rank_extent + 16, :].astype(jnp.float32)[0:1, :]
+        return jnp.where(own_slot == s.astype(jnp.float32), here, rank)
+
+    rank = lax.fori_loop(0, 2 * n, find_rank, jnp.ones((rows, rank_extent), jnp.float32))
+    feature = lax.broadcasted_iota(jnp.int32, (rows, rank_extent), 1).astype(jnp.float32)
+    shrink = total[part_of(place, rows), :]
+    for k in range(1, group):
+        coming(total_copy, k).wait_recv()
+        shrink = shrink + totals_got[flip(place, k)]
+    low_got[place] = jnp.where(feature < rank, shrink * lax.rsqrt(rank), 0.0).astype(jnp.bfloat16)
+    for k in range(1, group):
+        sent(low_copy, k).start()
+
+    def expand_block(j):
+        slot = slots_got[part_of(j, rows), :].astype(jnp.float32)
+        low = low_got[j].astype(jnp.float32)
+
+        def pair(s, sum_so_far):
+            low_slot = (2 * s).astype(jnp.float32)
+            spread = jnp.concatenate(
+                [
+                    jnp.where(slot == low_slot, low, 0.0).astype(jnp.bfloat16),
+                    jnp.where(slot == low_slot + 1.0, low, 0.0).astype(jnp.bfloat16),
+                ],
+                axis=1,
+            )
+            weight = jnp.concatenate(
+                [up_got[2 * s, :rank_extent, :], up_got[2 * s + 1, :rank_extent, :]], axis=0
+            )
+            return sum_so_far + jnp.dot(spread, weight, preferred_element_type=jnp.float32)
+
+        delta[j] = lax.fori_loop(
+            0, n, pair, jnp.zeros((rows, keys), jnp.float32), unroll=4
+        ).astype(jnp.bfloat16)
+
+    def expand_step(k, carry):
+        coming(low_copy, k).wait_recv()
+        expand_block(flip(place, k))
+        sent(delta_copy, k).start()
+        return carry
+
+    def rotate(j, values):
+        at = part_of(j, keys)
+        pre = base[:, at] + values.astype(jnp.float32)
+        turned = pltpu.roll(pre, keys // 2, axis=1)
+        out[:, at] = (pre * cosine[...] + turned * sine[...]).astype(out.dtype)
+
+    def rotate_step(k, carry):
+        coming(delta_copy, k).wait_recv()
+        j = flip(place, k)
+        rotate(j, delta_got[j])
+        return carry
+
+    lax.fori_loop(1, group, expand_step, 0)
+    expand_block(place)
+    rotate(place, delta[place])
+    lax.fori_loop(1, group, rotate_step, 0)
+
+    for k in range(1, group):
+        for copy in (hidden_copy, slots_copy, total_copy, low_copy, delta_copy):
+            sent(copy, k).wait_send()
+    for k in range(1, n):
+        if k < 4:
+            sent(near_copy, k).wait_send()
+        else:
+            sent(down_copy, k).wait_send()
+            down_pass(k, part).wait_send()
+        sent(up_copy, k).wait_send()
+        up_pass(k, part).wait_send()
+
+
+def keys_call(hidden, key_weight, down, up, slots, cosine, sine):
+    n = lax.axis_size("rep")
+    group = n // 2
+    rows, features = hidden.shape
+    rank_extent = down.shape[2]
+    width = features // group
+    keys = key_weight.shape[1]
+    key_block = keys // group
+    any_space = pl.BlockSpec(memory_space=pl.ANY)
+    vmem = pl.BlockSpec(memory_space=pltpu.VMEM)
+    half, full = jnp.bfloat16, jnp.float32
+    dma = pltpu.SemaphoreType.DMA
+    return pl.pallas_call(
+        functools.partial(keys_kernel, n, group),
+        out_shape=jax.ShapeDtypeStruct((rows, keys), half),
+        in_specs=[any_space] * 5 + [vmem] * 2,
+        out_specs=vmem,
+        scratch_shapes=[
+            pltpu.VMEM((rows, features), half),
+            pltpu.VMEM((features, keys), half),
+            pltpu.VMEM((group * rows, width), half),
+            pltpu.VMEM((group * rows, rank_extent), half),
+            pltpu.VMEM((2 * n, width, rank_extent), half),
+            pltpu.VMEM((2 * n, up.shape[1], key_block), half),
+            pltpu.VMEM((rows, keys), full),
+            pltpu.VMEM((group * rows, rank_extent), full),
+            pltpu.VMEM((group, rows, rank_extent), full),
+            pltpu.VMEM((group, rows, rank_extent), half),
+            pltpu.VMEM((group, rows, key_block), half),
+            pltpu.VMEM((group, rows, key_block), half),
+        ]
+        + [dma((group,))] * 4
+        + [dma((n,))] * 8
+        + [dma((group,))] * 6
+        + [dma((5,)), dma((n,))],
+        compiler_params=pltpu.CompilerParams(
+            collective_id=0, has_side_effects=True, vmem_limit_bytes=56 * 2**20
+        ),
+        cost_estimate=pl.CostEstimate(
+            flops=2 * rows * features * keys + 4 * rows * features * n * rank_extent,
+            bytes_accessed=2 * features * (rows + keys + 2 * rank_extent),
+            transcendentals=0,
+        ),
+    )(hidden, key_weight, down, up, slots, cosine, sine)
+
+
+def shared(
+    hidden,
+    request_adapter,
+    lengths,
+    key_projection_weight,
+    adapter_down_weight,
+    adapter_up_weight,
+    slot_adapter_rank,
+    placement,
+):
+    rows = hidden.shape[0]
+    adapters = placement.shape[0]
+    rank_extent = adapter_down_weight.shape[2]
+    numbers = jnp.arange(adapters, dtype=jnp.int32)[None, :]
+    slot_ids = jnp.sum(jnp.where(request_adapter == numbers, placement[None, :], 0), axis=1)
+    slots = jnp.broadcast_to(slot_ids[:, None].astype(jnp.bfloat16), (rows, rank_extent))
+    ranks = jnp.broadcast_to(
+        slot_adapter_rank.astype(jnp.bfloat16)[:, None, None],
+        (slot_adapter_rank.shape[0], 16, adapter_up_weight.shape[2]),
+    )
+    up = jnp.concatenate([adapter_up_weight, ranks], axis=1)
+    half_size = HEAD // 2
+    inverse = jnp.exp(
+        jnp.arange(half_size, dtype=jnp.float32) * (-2.0 * math.log(10000.0) / HEAD)
+    )
+    angles = lengths.astype(jnp.float32)[:, None] * inverse[None, :]
+    cosine, sine = jnp.cos(angles), jnp.sin(angles)
+    return keys_call(
+        hidden,
+        key_projection_weight,
+        adapter_down_weight,
+        up,
+        slots,
+        jnp.concatenate([cosine, cosine], axis=1),
+        jnp.concatenate([-sine, sine], axis=1),
+    )
+
+
 def solution(mesh):
+    sizes = dict(mesh.shape)
+    fits = sizes["parts"] == 2 and sizes["tp"] == 1 and sizes["rep"] == 16
+    on_device = shared if fits else routed
     in_specs = (
         P(("parts", "rep"), "tp"),
         P(("parts", "rep"), None),

time: 360 us -> 196 us (0.54)
  the two profiles are of different devices: /device:TPU:13 before, /device:TPU:3 now
where the time goes in v2:
time: 196 us
  Pallas kernels  188 us (96%)
  other arithmetic  5.39 us (3%)
  local copies, waits for them, and re-layouts  2.66 us (1%)
    pallas_call x1, Pallas kernels, keys_call(): pl.pallas_call(functools.partial(keys_kernel, n, group), out_shape=jax.Sh...  188 us

profile of v2, /device:TPU:3, one launch (start us, length us, event | category | flops | bytes accessed | tf_op | source)
XLA Modules:
  0.0 196.0 jit_solution(12278650408554336749)
XLA Ops:
  0.0 0.7 convert_element_type.14
  0.7 0.8 select_reduce_fusion
  1.5 0.7 convert_element_type.16
  2.1 0.7 broadcast_in_dim.19.slots
  2.9 0.1 broadcast_in_dim.16
  2.9 0.5 fusion
  3.5 0.8 pad_maximum_fusion.1
  4.3 1.9 pad_maximum_fusion.up
  6.2 188.0 %shard_map.82 = bf16[256,1024]{1,0:T(8,128)(2,1)} custom-call(bf16[256,8192]{1,0:T(8,128)(2,1)} %hidden.1, bf16[8192,1024]{1,0:T(8,128)(2,1)} %key_weight.1, bf16[2,8192,128]{2,1,0:T(8,128)(2,1)} %down.1, bf16[2,144,1024]{2,1,0:T(8,128)(2,1)} %pad_maximum_fusion.up, bf16[256,128]{1,0:T(8,128)(2,1)} %broadcast_in_dim.19.slots, ...), custom_call_target="tpu_custom_call" | custom-call | flops 21474836480 | bytes 25165824 | tf_op jit(solution)/shard_map/pallas_call | solution.py:511
  194.2 1.9 copy.10
  (2 shorter events, 0.0 us)

commit v3 on v2

--- a/solution.py
+++ b/solution.py
@@ -100,7 +100,7 @@
 MESH = pl.DeviceIdType.MESH
 WINDOW = 4
 TILE = 1024
-TURN = 9
+TURN = 11
 
 
 def flip(index, mask):

time: 196 us -> 193 us (0.985)
  the two profiles are of different devices: /device:TPU:3 before, /device:TPU:13 now
where the time goes in v3:
time: 193 us; the launch traced here: 191 us
  Pallas kernels  183 us (95%)
  other arithmetic  5.39 us (3%)
  local copies, waits for them, and re-layouts  2.66 us (1%)
    pallas_call x1, Pallas kernels, keys_call(): pl.pallas_call(functools.partial(keys_kernel, n, group), out_shape=jax.Sh...  183 us

profile of v3, /device:TPU:13, one launch (start us, length us, event | category | flops | bytes accessed | tf_op | source)
XLA Modules:
  0.0 191.3 jit_solution(4966361137968988630)
XLA Ops:
  0.0 0.7 convert_element_type.14
  0.7 0.8 select_reduce_fusion
  1.5 0.7 convert_element_type.16
  2.1 0.7 broadcast_in_dim.19.slots
  2.9 0.1 broadcast_in_dim.16
  2.9 0.5 fusion
  3.5 0.8 pad_maximum_fusion.1
  4.3 1.9 pad_maximum_fusion.up
  6.2 183.2 %shard_map.82 = bf16[256,1024]{1,0:T(8,128)(2,1)} custom-call(bf16[256,8192]{1,0:T(8,128)(2,1)} %hidden.1, bf16[8192,1024]{1,0:T(8,128)(2,1)} %key_weight.1, bf16[2,8192,128]{2,1,0:T(8,128)(2,1)} %down.1, bf16[2,144,1024]{2,1,0:T(8,128)(2,1)} %pad_maximum_fusion.up, bf16[256,128]{1,0:T(8,128)(2,1)} %broadcast_in_dim.19.slots, ...), custom_call_target="tpu_custom_call" | custom-call | flops 21474836480 | bytes 25165824 | tf_op jit(solution)/shard_map/pallas_call | solution.py:511
  189.4 1.9 copy.10
  (2 shorter events, 0.0 us)
